TPU v7x, 512 devices: a whole 4x4x16 slice. The times are simulated.
512 devices in a mesh: tm: 8 (over z_lo), height: 64 (over z_hi, y, x, core).
Axes of the slice: x: 4, y: 4, z: 16 (z_hi: 2, z_lo: 8; z = z_hi * 8 + z_lo), core: 2. Of those that a mesh axis runs over, the one named last changes fastest.
Arguments:
- features: bfloat16 [16, 512, 32, 512], P('tm', 'height'), may hold values from -6 to 6
- clip_frames: int32 [4], replicated, may hold values from 1 to 7, 16 in all
- conv_mid: bfloat16 [3, 3, 3, 512, 512], replicated, may hold values from -0.0546875 to 0.0546875
- bias_mid: float32 [512], replicated, may hold values from -3 to 3
- conv_latent: bfloat16 [3, 3, 3, 512, 16], replicated, may hold values from -0.0546875 to 0.0546875
- bias_latent: float32 [16], replicated, may hold values from -4 to 4
- patch_weight: bfloat16 [64, 3072], replicated, may hold values from -0.75 to 0.75
- patch_bias: float32 [3072], replicated, may hold values from -3 to 3
Outputs:
- embedded: bfloat16 [65536, 3072], P(('tm', 'height'))
Inputs may be any that keep to these rules, and one draw needn't show every extreme that they name: `clip_frames`: latent frames of each clip in packing order; they sum to 16, and the longest clip has exactly 7.
All inputs are finite; a program needn't handle non-finite values.
Results may differ from a plain program's by a relative error of at most 0.0075.
Values may be sent and summed in bfloat16 or wider, within the bound.
A program may use at most 128 MiB of HBM per device.

v0:
```python
import jax
import jax.numpy as jnp
import numpy as np
from jax import lax
from jax.sharding import PartitionSpec as P

latent_scale = 0.476986


def passed_along(x, axis, by):
    count = lax.axis_size(axis)
    pairs = [(i, i + by) for i in range(count) if 0 <= i + by < count]
    return lax.ppermute(x, axis, pairs)


def padded_2(cells, sides, width):
    for axis, dim in sides:
        count = lax.axis_size(axis)
        ends = count - 1
        head = lax.slice_in_dim(cells, 0, width, axis=dim)
        tail = lax.slice_in_dim(cells, cells.shape[dim] - width, cells.shape[dim], axis=dim)
        cells = jnp.concatenate(
            [
                lax.ppermute(tail, axis, [(i, (i + 1) % count) for i in range(ends)]),
                cells,
                lax.ppermute(head, axis, [((i + 1) % count, i) for i in range(ends)]),
            ],
            axis=dim,
        )
    return cells


def source_lags(clip_frames, first_frame, frame_total):
    clip_starts = jnp.cumsum(clip_frames, dtype=jnp.int32) - clip_frames
    frame_index = first_frame + jnp.arange(frame_total, dtype=jnp.int32)
    clip_begin = jnp.max(
        jnp.where(clip_starts[None, :] <= frame_index[:, None], clip_starts[None, :], 0), axis=1
    )
    back_steps = jnp.arange(3, dtype=jnp.int32)
    return jnp.minimum(back_steps[:, None], (frame_index - clip_begin)[None, :])


def frame_columns(block):
    row_count = block.shape[-3] - 2
    col_count = block.shape[-2]
    pad_widths = [(0, 0)] * (block.ndim - 2) + [(1, 1), (0, 0)]
    padded = jnp.pad(block, pad_widths)
    pieces = [
        padded[..., row_shift : row_shift + row_count, col_shift : col_shift + col_count, :]
        for row_shift in range(3)
        for col_shift in range(3)
    ]
    return jnp.concatenate(pieces, axis=-1)


def window_edges(padded):
    band_count = lax.axis_size("height")
    band_index = lax.axis_index("height")
    row_index = jnp.arange(padded.shape[1], dtype=jnp.int32)
    keep_top = band_index % band_count != 0
    keep_bottom = band_index % band_count != band_count - 1
    keep_rows = jnp.where(
        row_index == 0, keep_top, jnp.where(row_index == padded.shape[1] - 1, keep_bottom, True)
    )
    return jnp.where(keep_rows[None, :, None, None], padded, jnp.zeros_like(padded))


def extend_block(activated):
    previous = passed_along(activated, "tm", 1)
    joined = jnp.concatenate([previous, activated], axis=0)
    return window_edges(padded_2(joined, (("height", 1),), 1))


def select_sources(extended, lag_row, slab_frames, reach):
    picked = extended[2 : 2 + slab_frames]
    for source_lag in range(1, reach + 1):
        chosen_rows = (lag_row == source_lag)[:, None, None, None]
        picked = jnp.where(
            chosen_rows, extended[2 - source_lag : 2 - source_lag + slab_frames], picked
        )
    return picked


def lagged_sum(extended, taps, lags):
    slab_frames = extended.shape[0] - 2
    columns = frame_columns(extended)
    summed = None
    for back_step in range(3):
        picked = select_sources(columns, lags[back_step], slab_frames, back_step)
        term = jnp.einsum(
            "fhwk,ko->fhwo", picked, taps[back_step], preferred_element_type=jnp.float32
        )
        summed = term if summed is None else summed + term
    return summed


def per_device(
    features, clip_frames, conv_mid, bias_mid, conv_latent, bias_latent, patch_weight, patch_bias
):
    slab_frames, band_rows, col_count, channels = features.shape
    latent_width = conv_latent.shape[-1]
    lags = source_lags(clip_frames, lax.axis_index("tm") * slab_frames, slab_frames)
    taps_mid = conv_mid.reshape(3, 9 * channels, channels)
    taps_latent = conv_latent.reshape(3, 9 * channels, latent_width)
    act_first = jax.nn.silu(features.astype(jnp.float32)).astype(jnp.bfloat16)
    mixed = lagged_sum(extend_block(act_first), taps_mid, lags)
    hidden = (features.astype(jnp.float32) + mixed + bias_mid).astype(jnp.bfloat16)
    hidden = lax.optimization_barrier(hidden)
    act_second = jax.nn.silu(hidden.astype(jnp.float32)).astype(jnp.bfloat16)
    raw_latent = lagged_sum(extend_block(act_second), taps_latent, lags)
    latent = (raw_latent + bias_latent) * latent_scale
    grid = latent.reshape(
        slab_frames, band_rows // 2, 2, col_count // 2, 2, latent_width
    ).transpose(0, 3, 1, 5, 2, 4)
    flat_patches = grid.reshape(
        slab_frames * (col_count // 2) * (band_rows // 2), 4 * latent_width
    ).astype(jnp.bfloat16)
    band_count = lax.axis_size("height")
    band_index = lax.axis_index("height")
    senders = min(band_count, slab_frames * col_count // 2)
    spacing = band_count // senders
    targets = band_count // spacing
    capacity = flat_patches.shape[0] // targets
    blocks = flat_patches.reshape(targets, capacity, 4 * latent_width)
    target_index = jnp.asarray(np.arange(targets) * spacing, jnp.int32) + band_index // senders
    outgoing = (
        jnp.zeros((band_count, capacity, 4 * latent_width), jnp.bfloat16)
        .at[target_index]
        .set(blocks)
    )
    first_source = band_index * senders % band_count
    sources = lax.dynamic_slice_in_dim(
        lax.all_to_all(outgoing, "height", split_axis=0, concat_axis=0, tiled=True),
        first_source,
        senders,
        0,
    )
    product = jnp.einsum("jpk,kd->jpd", sources, patch_weight, preferred_element_type=jnp.float32)
    embedded = (product + patch_bias).astype(jnp.bfloat16)
    column_groups = capacity // (band_rows // 2)
    ordered = embedded.reshape(
        senders, column_groups, band_rows // 2, embedded.shape[-1]
    ).transpose(1, 0, 2, 3)
    return ordered.reshape(-1, embedded.shape[-1])


def solution(mesh):
    return jax.shard_map(
        per_device,
        mesh=mesh,
        in_specs=(P("tm", "height", None, None), P(), P(), P(), P(), P(), P(), P()),
        out_specs=P(("tm", "height"), None),
        check_vma=False,
    )
```

profile of v0, /device:TPU:1, one launch (start us, length us, event | category | flops | bytes accessed | tf_op | source)
XLA Modules:
  0.0 141.7 jit_solution(3994069540092582393)
XLA Ops:
  0.0 1.4 fusion.52
  1.4 4.4 %collective-permute-start = (bf16[2,8,32,512]{3,2,1,0:T(8,128)(2,1)S(1)}, bf16[2,8,32,512]{3,2,1,0:T(8,128)(2,1)S(1)}, u32[]{:S(2)}, u32[]{:S(2)}) collective-permute-start(bf16[2,8,32,512]{3,2,1,0:T(8,128)(2,1)S(1)} %fusion.52), channel_id=1, source_target_pairs={{0,64},{64,128},{128,192},{192,256},{256,320},{320,384},{384,448},... | collective-permute-start | bytes 1572872 | tf_op jit(solution)/shard_map/ppermute | solution.py:13
  5.8 0.8 reduce-window.9
  6.7 0.7 bitcast_subtract_fusion
  7.3 0.2 fusion.58
  7.5 10.7 %fusion.60 = (bf16[1,3,3,512,512]{4,3,2,1,0:T(8,128)(2,1)}, bf16[1,3,3,512,512]{4,3,2,1,0:T(8,128)(2,1)}, bf16[1,3,3,512,512]{4,3,2,1,0:T(8,128)(2,1)}) fusion(bf16[3,3,3,512,512]{4,3,2,1,0:T(8,128)(2,1)} %param.11), kind=kLoop, calls=%fused_computation.102 | loop fusion | bytes 28311552 | tf_op jit(solution)/shard_map/slice | solution.py:91
  18.3 4.0 %collective-permute-start.1 = (bf16[4,1,32,512]{3,2,1,0:T(8,128)(2,1)S(1)}, bf16[4,1,32,512]{3,2,1,0:T(8,128)(2,1)S(1)}, u32[]{:S(2)}, u32[]{:S(2)}) collective-permute-start(bf16[4,1,32,512]{3,2,1,0:T(8,128)(2,1)S(1)} %get-tuple-element.10), channel_id=1, source_target_pairs={{0,1},{1,2},{2,3},{3,4},{4,5},{5,6},{6,7},{7,8},{8,9},{9,10},{10,1... | collective-permute-start | bytes 393224 | tf_op jit(solution)/shard_map/ppermute | solution.py:24
  22.2 3.0 %collective-permute-start.2 = (bf16[4,1,32,512]{3,2,1,0:T(8,128)(2,1)S(1)}, bf16[4,1,32,512]{3,2,1,0:T(8,128)(2,1)S(1)}, u32[]{:S(2)}, u32[]{:S(2)}) collective-permute-start(bf16[4,1,32,512]{3,2,1,0:T(8,128)(2,1)S(1)} %get-tuple-element.11), channel_id=1, source_target_pairs={{1,0},{2,1},{3,2},{4,3},{5,4},{6,5},{7,6},{8,7},{9,8},{10,9},{11,1... | collective-permute-start | bytes 393224 | tf_op jit(solution)/shard_map/ppermute | solution.py:26
  25.4 3.2 %collective-permute-done.2 = bf16[4,1,32,512]{3,2,1,0:T(8,128)(2,1)S(1)} collective-permute-done((bf16[4,1,32,512]{3,2,1,0:T(8,128)(2,1)S(1)}, bf16[4,1,32,512]{3,2,1,0:T(8,128)(2,1)S(1)}, u32[]{:S(2)}, u32[]{:S(2)}) %collective-permute-start.2) | collective-permute-done | bytes 131104 | tf_op jit(solution)/shard_map/ppermute | solution.py:26
  28.5 0.3 maximum_select_fusion
  28.8 0.3 fusion.37
  29.3 0.5 fusion.38
  29.7 0.5 fusion.39
  30.3 0.5 fusion.40
  30.8 0.5 fusion.41
  31.4 0.5 fusion.42
  31.9 2.6 %fusion.62 = f32[2,8,32,512]{3,2,1,0:T(8,128)S(1)} fusion(bf16[4,8,32,4608]{3,2,1,0:T(8,128)(2,1)S(1)} %fusion.42, bf16[4608,512,1,1]{1,0,3,2:T(8,128)(2,1)S(1)} %bitcast.60), kind=kOutput, calls=%fused_computation.104 | convolution fusion | flops 2415919104 | bytes 15204352 | tf_op jit(solution)/shard_map/fhwk,ko->fhwo/dot_general | solution.py:90
  34.6 2.6 %fusion.24 = f32[2,8,32,512]{3,2,1,0:T(8,128)S(1)} fusion(f32[2,8,32,512]{3,2,1,0:T(8,128)S(1)} %fusion.62, bf16[4608,512,1,1]{1,0,3,2:T(8,128)(2,1)S(1)} %bitcast.57, pred[2]{0:T(512)(128)(4,1)S(1)} %get-tuple-element.17, bf16[4,8,32,4608]{3,2,1,0:T(8,128)(2,1)S(1)} %fusion.42), kind=kOutput, calls=%fused_computation.43 | convolution fusion | flops 2418540544 | bytes 16252930 | tf_op jit(solution)/shard_map/fhwk,ko->fhwo/dot_general | solution.py:90
  37.3 2.9 %fusion.28 = bf16[2,8,32,512]{3,2,1,0:T(8,128)(2,1)S(1)} fusion(f32[2,8,32,512]{3,2,1,0:T(8,128)S(1)} %fusion.24, bf16[4608,512,1,1]{1,0,3,2:T(8,128)(2,1)S(1)} %bitcast.54, bf16[4,8,32,4608]{3,2,1,0:T(8,128)(2,1)S(1)} %fusion.42, pred[2]{0:T(512)(128)(4,1)S(1)} %get-tuple-element.16, pred[2]{0:T(512)(128)(4,1)S(1)} %get-tuple-element.15, ...), kind=kOutput, calls=%fused_computation.49 | convolution fusion | flops 2421948416 | bytes 20974592 | tf_op jit(solution)/shard_map/fhwk,ko->fhwo/dot_general | solution.py:90
  40.2 0.3 fusion.36
  40.5 3.5 %collective-permute-start.3 = (bf16[2,8,32,512]{3,2,1,0:T(8,128)(2,1)S(1)}, bf16[2,8,32,512]{3,2,1,0:T(8,128)(2,1)S(1)}, u32[]{:S(2)}, u32[]{:S(2)}) collective-permute-start(bf16[2,8,32,512]{3,2,1,0:T(8,128)(2,1)S(1)} %fusion.36), channel_id=1, source_target_pairs={{0,64},{64,128},{128,192},{192,256},{256,320},{320,384},{384,448},... | collective-permute-start | bytes 1572872 | tf_op jit(solution)/shard_map/ppermute | solution.py:13
  44.1 13.3 %collective-permute-done.3 = bf16[2,8,32,512]{3,2,1,0:T(8,128)(2,1)S(1)} collective-permute-done((bf16[2,8,32,512]{3,2,1,0:T(8,128)(2,1)S(1)}, bf16[2,8,32,512]{3,2,1,0:T(8,128)(2,1)S(1)}, u32[]{:S(2)}, u32[]{:S(2)}) %collective-permute-start.3) | collective-permute-done | bytes 524320 | tf_op jit(solution)/shard_map/ppermute | solution.py:13
  57.5 1.9 %collective-permute-start.4 = (bf16[4,1,32,512]{3,2,1,0:T(8,128)(2,1)S(1)}, bf16[4,1,32,512]{3,2,1,0:T(8,128)(2,1)S(1)}, u32[]{:S(2)}, u32[]{:S(2)}) collective-permute-start(bf16[4,1,32,512]{3,2,1,0:T(8,128)(2,1)S(1)} %get-tuple-element.8), channel_id=1, source_target_pairs={{0,1},{1,2},{2,3},{3,4},{4,5},{5,6},{6,7},{7,8},{8,9},{9,10},{10,1... | collective-permute-start | bytes 393224 | tf_op jit(solution)/shard_map/ppermute | solution.py:24
  59.4 2.6 %collective-permute-start.5 = (bf16[4,1,32,512]{3,2,1,0:T(8,128)(2,1)S(1)}, bf16[4,1,32,512]{3,2,1,0:T(8,128)(2,1)S(1)}, u32[]{:S(2)}, u32[]{:S(2)}) collective-permute-start(bf16[4,1,32,512]{3,2,1,0:T(8,128)(2,1)S(1)} %get-tuple-element.9), channel_id=1, source_target_pairs={{1,0},{2,1},{3,2},{4,3},{5,4},{6,5},{7,6},{8,7},{9,8},{10,9},{11,1... | collective-permute-start | bytes 393224 | tf_op jit(solution)/shard_map/ppermute | solution.py:26
  62.0 0.1 copy.31
  62.2 0.2 reshape.105
  62.5 0.2 reshape.106
  62.9 0.2 reshape.104
  63.1 2.6 %collective-permute-done.5 = bf16[4,1,32,512]{3,2,1,0:T(8,128)(2,1)S(1)} collective-permute-done((bf16[4,1,32,512]{3,2,1,0:T(8,128)(2,1)S(1)}, bf16[4,1,32,512]{3,2,1,0:T(8,128)(2,1)S(1)}, u32[]{:S(2)}, u32[]{:S(2)}) %collective-permute-start.5) | collective-permute-done | bytes 131104 | tf_op jit(solution)/shard_map/ppermute | solution.py:26
  65.7 0.3 maximum_select_fusion.1
  65.9 0.3 fusion.43
  66.4 0.5 fusion.44
  66.9 0.5 fusion.45
  67.5 0.5 fusion.46
  67.9 0.5 fusion.47
  68.6 0.5 fusion.48
  69.0 3.4 %fusion.3 = f32[2,8,32,16]{2,3,1,0:T(8,128)S(1)} fusion(pred[2]{0:T(512)(128)(4,1)S(1)} %get-tuple-element.17, bf16[4,8,32,4608]{3,2,1,0:T(8,128)(2,1)S(1)} %fusion.48, bf16[4608,16,1,1]{0,1,2,3:T(8,128)(2,1)S(1)} %reshape.105), kind=kOutput, calls=%fused_computation.6 | convolution fusion | flops 77856768 | bytes 9617410 | tf_op jit(solution)/shard_map/fhwk,ko->fhwo/dot_general | solution.py:90
  72.4 3.4 %fusion = f32[2,8,32,16]{2,3,1,0:T(8,128)S(1)} fusion(bf16[4,8,32,4608]{3,2,1,0:T(8,128)(2,1)S(1)} %fusion.48, pred[2]{0:T(512)(128)(4,1)S(1)} %get-tuple-element.16, pred[2]{0:T(512)(128)(4,1)S(1)} %get-tuple-element.15, bf16[4608,16,1,1]{0,1,2,3:T(8,128)(2,1)S(1)} %reshape.106), kind=kOutput, calls=%fused_computation.2 | convolution fusion | flops 80216064 | bytes 14337024 | tf_op jit(solution)/shard_map/fhwk,ko->fhwo/dot_general | solution.py:90
  75.9 3.2 %fusion.32 = bf16[2,8,32,16]{2,3,1,0:T(8,128)(2,1)S(1)} fusion(f32[2,8,32,16]{2,3,1,0:T(8,128)S(1)} %fusion, f32[2,8,32,16]{2,3,1,0:T(8,128)S(1)} %fusion.3, bf16[4,8,32,4608]{3,2,1,0:T(8,128)(2,1)S(1)} %fusion.48, bf16[4608,16,1,1]{0,1,2,3:T(8,128)(2,1)S(1)} %reshape.104, f32[16]{0:T(128)S(1)} %copy-done.4), kind=kOutput, calls=%fused_computation.54 | convolution fusion | flops 75538432 | bytes 9666624 | tf_op jit(solution)/shard_map/fhwk,ko->fhwo/dot_general | solution.py:90
  79.1 0.1 copy.33
  79.2 0.1 copy.34
  79.6 1.5 %scatter_fusion = bf16[64,4,64]{2,1,0:T(4,128)(2,1)S(1)} fusion(bf16[64,4,64]{2,1,0:T(4,128)(2,1)S(1)} %broadcast_in_dim.85, s32[32]{0:T(128)S(1)} %compare_select_fusion, bf16[32,4,64]{2,1,0:T(4,128)(2,1)S(1)} %copy.35), kind=kCustom, calls=%fused_computation | custom fusion | bytes 49280 | tf_op jit(solution)/shard_map/scatter | solution.py:129
  81.1 0.7 reshape.111
  81.8 41.2 %all-to-all-start = ((bf16[64,2,128]{2,1,0:T(2,128)(2,1)}), bf16[64,2,128]{2,1,0:T(2,128)(2,1)S(1)}, u32[]{:S(2)}, u32[]{:S(2)}) async-start(bf16[64,2,128]{2,1,0:T(2,128)(2,1)} %reshape.111), calls=%async_computation | async-start | bytes 65536 | tf_op jit(solution)/shard_map/all_to_all | solution.py:133
  123.0 16.5 %all-to-all-done = bf16[64,2,128]{2,1,0:T(2,128)(2,1)S(1)} async-done(((bf16[64,2,128]{2,1,0:T(2,128)(2,1)}), bf16[64,2,128]{2,1,0:T(2,128)(2,1)S(1)}, u32[]{:S(2)}, u32[]{:S(2)}) %all-to-all-start) | async-done | bytes 32800 | tf_op jit(solution)/shard_map/all_to_all | solution.py:133
  139.6 0.3 fusion.22
  140.0 0.6 copy.37
  140.6 1.1 reshape_transpose_reshape.3
  (52 shorter events, 1.4 us)
Async XLA Ops:
  0.0 139.6 %copy-start = (bf16[64,3072]{1,0:T(8,128)(2,1)S(1)}, bf16[64,3072]{1,0:T(8,128)(2,1)}, u32[]{:S(2)}) copy-start(bf16[64,3072]{1,0:T(8,128)(2,1)} %param.15) | copy-start | bytes 1179652
  1.4 16.8 %collective-permute-start = (bf16[2,8,32,512]{3,2,1,0:T(8,128)(2,1)S(1)}, bf16[2,8,32,512]{3,2,1,0:T(8,128)(2,1)S(1)}, u32[]{:S(2)}, u32[]{:S(2)}) collective-permute-start(bf16[2,8,32,512]{3,2,1,0:T(8,128)(2,1)S(1)} %fusion.52), channel_id=1, source_target_pairs={{0,64},{64,128},{128,192},{192,256},{256,320},{320,384},{384,448},... | collective-permute-start | bytes 1572872 | tf_op jit(solution)/shard_map/ppermute | solution.py:13
  18.3 7.1 %collective-permute-start.1 = (bf16[4,1,32,512]{3,2,1,0:T(8,128)(2,1)S(1)}, bf16[4,1,32,512]{3,2,1,0:T(8,128)(2,1)S(1)}, u32[]{:S(2)}, u32[]{:S(2)}) collective-permute-start(bf16[4,1,32,512]{3,2,1,0:T(8,128)(2,1)S(1)} %get-tuple-element.10), channel_id=1, source_target_pairs={{0,1},{1,2},{2,3},{3,4},{4,5},{5,6},{6,7},{7,8},{8,9},{9,10},{10,1... | collective-permute-start | bytes 393224 | tf_op jit(solution)/shard_map/ppermute | solution.py:24
  22.2 6.3 %collective-permute-start.2 = (bf16[4,1,32,512]{3,2,1,0:T(8,128)(2,1)S(1)}, bf16[4,1,32,512]{3,2,1,0:T(8,128)(2,1)S(1)}, u32[]{:S(2)}, u32[]{:S(2)}) collective-permute-start(bf16[4,1,32,512]{3,2,1,0:T(8,128)(2,1)S(1)} %get-tuple-element.11), channel_id=1, source_target_pairs={{1,0},{2,1},{3,2},{4,3},{5,4},{6,5},{7,6},{8,7},{9,8},{10,9},{11,1... | collective-permute-start | bytes 393224 | tf_op jit(solution)/shard_map/ppermute | solution.py:26
  29.2 2.6 %slice-start.4 = ((s8[4718592]{0:T(1024)(128)(4,1)}), s8[4194304]{0:T(1024)(128)(4,1)S(1)}, s32[]{:S(2)}) async-start(s8[4718592]{0:T(1024)(128)(4,1)} %bitcast.58), calls=%async_computation.5 | async-start | bytes 8388608
  30.3 1.6 %slice-start.5 = ((s8[4718592]{0:T(1024)(128)(4,1)}), s8[524288]{0:T(1024)(128)(4,1)S(1)}, s32[]{:S(2)}) async-start(s8[4718592]{0:T(1024)(128)(4,1)} %bitcast.58), calls=%async_computation.6 | async-start | bytes 1048576
  31.4 3.1 %slice-start.2 = ((s8[4718592]{0:T(1024)(128)(4,1)}), s8[4194304]{0:T(1024)(128)(4,1)S(1)}, s32[]{:S(2)}) async-start(s8[4718592]{0:T(1024)(128)(4,1)} %bitcast.55), calls=%async_computation.3 | async-start | bytes 8388608
  31.9 2.6 %slice-start.3 = ((s8[4718592]{0:T(1024)(128)(4,1)}), s8[524288]{0:T(1024)(128)(4,1)S(1)}, s32[]{:S(2)}) async-start(s8[4718592]{0:T(1024)(128)(4,1)} %bitcast.55), calls=%async_computation.4 | async-start | bytes 1048576
  31.9 5.3 %slice-start = ((s8[4718592]{0:T(1024)(128)(4,1)}), s8[4194304]{0:T(1024)(128)(4,1)S(1)}, s32[]{:S(2)}) async-start(s8[4718592]{0:T(1024)(128)(4,1)} %bitcast.52), calls=%async_computation.1 | async-start | bytes 8388608
  34.6 2.7 %slice-start.1 = ((s8[4718592]{0:T(1024)(128)(4,1)}), s8[524288]{0:T(1024)(128)(4,1)S(1)}, s32[]{:S(2)}) async-start(s8[4718592]{0:T(1024)(128)(4,1)} %bitcast.52), calls=%async_computation.2 | async-start | bytes 1048576
  34.6 2.7 %copy-start.1 = (bf16[2,8,32,512]{3,2,1,0:T(8,128)(2,1)S(1)}, bf16[2,8,32,512]{3,2,1,0:T(8,128)(2,1)}, u32[]{:S(2)}) copy-start(bf16[2,8,32,512]{3,2,1,0:T(8,128)(2,1)} %param.9) | copy-start | bytes 1572868
  34.6 2.7 %copy-start.5 = (f32[512]{0:T(512)S(1)}, f32[512]{0:T(512)}, u32[]{:S(2)}) copy-start(f32[512]{0:T(512)} %param.12) | copy-start | bytes 6148
  37.3 24.7 %copy-start.2 = (bf16[3,3,3,512,16]{3,4,2,1,0:T(8,128)(2,1)S(1)}, bf16[3,3,3,512,16]{3,4,2,1,0:T(8,128)(2,1)}, u32[]{:S(2)}) copy-start(bf16[3,3,3,512,16]{3,4,2,1,0:T(8,128)(2,1)} %param.13) | copy-start | bytes 1327108
  40.5 16.9 %collective-permute-start.3 = (bf16[2,8,32,512]{3,2,1,0:T(8,128)(2,1)S(1)}, bf16[2,8,32,512]{3,2,1,0:T(8,128)(2,1)S(1)}, u32[]{:S(2)}, u32[]{:S(2)}) collective-permute-start(bf16[2,8,32,512]{3,2,1,0:T(8,128)(2,1)S(1)} %fusion.36), channel_id=1, source_target_pairs={{0,64},{64,128},{128,192},{192,256},{256,320},{320,384},{384,448},... | collective-permute-start | bytes 1572872 | tf_op jit(solution)/shard_map/ppermute | solution.py:13
  57.5 5.7 %collective-permute-start.4 = (bf16[4,1,32,512]{3,2,1,0:T(8,128)(2,1)S(1)}, bf16[4,1,32,512]{3,2,1,0:T(8,128)(2,1)S(1)}, u32[]{:S(2)}, u32[]{:S(2)}) collective-permute-start(bf16[4,1,32,512]{3,2,1,0:T(8,128)(2,1)S(1)} %get-tuple-element.8), channel_id=1, source_target_pairs={{0,1},{1,2},{2,3},{3,4},{4,5},{5,6},{6,7},{7,8},{8,9},{9,10},{10,1... | collective-permute-start | bytes 393224 | tf_op jit(solution)/shard_map/ppermute | solution.py:24
  59.4 6.3 %collective-permute-start.5 = (bf16[4,1,32,512]{3,2,1,0:T(8,128)(2,1)S(1)}, bf16[4,1,32,512]{3,2,1,0:T(8,128)(2,1)S(1)}, u32[]{:S(2)}, u32[]{:S(2)}) collective-permute-start(bf16[4,1,32,512]{3,2,1,0:T(8,128)(2,1)S(1)} %get-tuple-element.9), channel_id=1, source_target_pairs={{1,0},{2,1},{3,2},{4,3},{5,4},{6,5},{7,6},{8,7},{9,8},{10,9},{11,1... | collective-permute-start | bytes 393224 | tf_op jit(solution)/shard_map/ppermute | solution.py:26
  72.4 3.4 %copy-start.4 = (f32[16]{0:T(128)S(1)}, f32[16]{0:T(128)}, u32[]{:S(2)}) copy-start(f32[16]{0:T(128)} %param.14) | copy-start | bytes 196
  75.9 63.7 %copy-start.3 = (f32[3072]{0:T(1024)S(1)}, f32[3072]{0:T(1024)}, u32[]{:S(2)}) copy-start(f32[3072]{0:T(1024)} %param.16) | copy-start | bytes 36868
  81.8 57.7 %all-to-all-start = ((bf16[64,2,128]{2,1,0:T(2,128)(2,1)}), bf16[64,2,128]{2,1,0:T(2,128)(2,1)S(1)}, u32[]{:S(2)}, u32[]{:S(2)}) async-start(bf16[64,2,128]{2,1,0:T(2,128)(2,1)} %reshape.111), calls=%async_computation | async-start | bytes 65536 | tf_op jit(solution)/shard_map/all_to_all | solution.py:133
where the time goes:
time: 144 us; the launch traced here: 142 us
  starting transfers between devices  60.6 us (42%)
  waiting for transfers between devices  35.5 us (25%)
  local copies, waits for them, and re-layouts  22.3 us (15%)
  matrix products  18.5 us (13%)
  other arithmetic  4.01 us (3%)
    all_to_all x1, starting transfers between devices, per_device(): lax.all_to_all(outgoing, 'height', split_axis=0, concat_axis=0, tiled=True)  41.2 us
    dot_general x6, matrix products, lagged_sum(): jnp.einsum('fhwk,ko->fhwo', picked, taps[back_step], preferred_element_ty...  18.2 us
    all_to_all x1, waiting for transfers between devices, per_device(): lax.all_to_all(outgoing, 'height', split_axis=0, concat_axis=0, tiled=True)  16.5 us
    ppermute x2, waiting for transfers between devices, passed_along(): return lax.ppermute(x, axis, pairs)  13.3 us
    slice x5, local copies, waits for them, and re-layouts, lagged_sum(): taps[back_step]  11.1 us
    ppermute x2, starting transfers between devices, passed_along(): return lax.ppermute(x, axis, pairs)  7.95 us
    unnamed x42, local copies, waits for them, and re-layouts  5.95 us
    ppermute x2, starting transfers between devices, padded_2(): lax.ppermute(tail, axis, [(i, (i + 1) % count) for i in range(ends)])  5.88 us
  transfers between devices with their start and end apart: 7, of which 4 were waited for; matrix products, arithmetic and copies ran while one was open for 10% of the time, Pallas kernels for 0%

commit v1 on v0

v1 whole, which is shorter than its diff:
```python
import functools

import jax
import jax.numpy as jnp
from jax import lax
from jax.experimental import pallas as pl
from jax.experimental.pallas import tpu as pltpu
from jax.sharding import PartitionSpec as P

latent_scale = 0.476986
MESH = pl.DeviceIdType.MESH
f32, bf16 = jnp.float32, jnp.bfloat16

PREV, EVEN, ODD, NEXT = range(4)
ROUTES = (
    (0, 0, 0, (0, 1, 2)),
    (1, 0, 1, (1, 2)),
    (1, 1, 0, (0, 1, 2)),
    (2, 0, 2, (2,)),
    (2, 1, 1, (1, 2)),
    (3, 1, 2, (2,)),
)


def device(s, zh, y, x, core):
    return (s, zh * 32 + y * 8 + x * 2 + core)


def kernel(
    x_hbm, clips_hbm, wm_hbm, bm_hbm, wl_hbm, bl_hbm, pw_hbm, pb_hbm, out_hbm,
    raw, act, shifted, wm, acc, late_raw, late, act2, wl, conv2, outgoing, incoming, patches, pw, pwp, out, bm, bl, pb, clips,
    sem_x, sem_w, sem_small, sem_out, send_main, recv_main, send_edge, recv_edge, send_patch, recv_patch, send_extra, recv_extra,
    know_plane, know_four, know_all,
):
    s, h = lax.axis_index("tm"), lax.axis_index("height")
    zh, y, x, core = h // 32, (h // 8) % 4, (h // 2) % 4, h % 2
    other = (h + 32) % 64
    z = zh * 8 + s

    def along_z(step):
        there = (z + step + 16) % 16
        return device(there % 8, there // 8, y, x, core)

    def above(step):
        band = (h + step + 64) % 64
        wrapped = (band + 32) % 64
        down = ((s + 7) % 8, jnp.where(s == 0, wrapped, band))
        up = ((s + 1) % 8, jnp.where(s == 7, wrapped, band))
        return (s, band), down, up

    has_top, has_bottom = h % 32 != 0, h % 32 != 31
    (_, down, up) = above(0)
    band_next = jnp.where(s == 7, other, h)
    band_prev = jnp.where(s == 0, other, h)

    load_x = pltpu.make_async_copy(x_hbm, raw.at[pl.ds(EVEN, 2), pl.ds(1, 8)], sem_x)
    load_x.start()
    load_w = [pltpu.make_async_copy(wm_hbm.at[k], wm.at[k], sem_w.at[k]) for k in range(3)]
    load_clips = pltpu.make_async_copy(clips_hbm, clips, sem_small.at[0])
    load_clips.start()
    load_w[0].start()

    line = [device(s, zh, y, (x + d) % 4, c) for d in (1, 2, 3) for c in (0, 1)] + [device(s, zh, y, x, 1 - core)]
    column = [device(s, zh, (y + d) % 4, x, core) for d in (1, 2, 3)]
    near_z = [along_z(d) for d in (-2, -1, 1, 2)]
    barrier = pltpu.get_barrier_semaphore()
    for there in line + column + near_z:
        pl.semaphore_signal(barrier, inc=1, device_id=there, device_id_type=MESH)

    @pl.when(has_top)
    def _():
        for there in above(-1):
            pl.semaphore_signal(barrier, inc=1, device_id=there, device_id_type=MESH)

    @pl.when(has_bottom)
    def _():
        for there in above(1):
            pl.semaphore_signal(barrier, inc=1, device_id=there, device_id_type=MESH)

    pl.semaphore_wait(barrier, 14 + 3 * has_top.astype(jnp.int32) + 3 * has_bottom.astype(jnp.int32))

    main = []
    for half in range(2):
        ch = pl.ds(half * 256, 256)
        for i, (frame, slot, there) in enumerate(((0, NEXT, down), (1, PREV, up))):
            main.append(
                pltpu.make_async_remote_copy(
                    x_hbm.at[frame, :, :, ch], raw.at[slot, pl.ds(1, 8), :, ch],
                    send_main.at[i, half], recv_main.at[i, half], device_id=there, device_id_type=MESH,
                )
            )

    def edge_copies(side, to_late):
        here, lower, upper = above(2 * side - 1)
        row, there_row = (0, 9) if side == 0 else (7, 0)
        copies = []
        for slot, frame, there in ((EVEN, 0, here), (ODD, 1, here), (NEXT, 0, lower), (PREV, 1, upper)):
            target = late_raw.at[slot] if to_late else raw.at[slot, there_row]
            copies.append(
                pltpu.make_async_remote_copy(
                    x_hbm.at[frame, row], target, send_edge.at[slot, side], recv_edge.at[slot, side],
                    device_id=there, device_id_type=MESH,
                )
            )
        return copies

    @pl.when(has_top)
    def _():
        for c in edge_copies(0, False):
            c.start()

    @pl.when(has_bottom)
    def _():
        for c in edge_copies(1, False):
            c.start()

    for c in main:
        c.start()
    for there in column + near_z:
        pl.semaphore_signal(know_plane, inc=1, device_id=there, device_id_type=MESH)
    load_w[1].start()
    load_w[2].start()
    small = [
        pltpu.make_async_copy(a, b, sem_small.at[1 + i])
        for i, (a, b) in enumerate(((bm_hbm, bm), (bl_hbm, bl), (pw_hbm, pw), (pb_hbm, pb)))
    ]
    for c in small:
        c.start()
    wl[...] = jnp.zeros_like(wl)
    tap_copies = [
        pltpu.make_async_copy(wl_hbm.at[k, i, j], wl.at[j, pl.ds(k * 128 + i * 16, 16)], sem_small.at[5 + k * 9 + i * 3 + j])
        for k in range(3) for i in range(3) for j in range(3)
    ]
    for c in tap_copies:
        c.start()

    shifted[:, 0:8] = jnp.zeros((10, 8, 256), f32)
    shifted[:, 40:48] = jnp.zeros((10, 8, 256), f32)
    late_raw_zero = jnp.zeros((32, 512), bf16)

    def silu(v):
        return v / (1.0 + jnp.exp(-v))

    def prepare(slot, half):
        ch = slice(half * 256, half * 256 + 256)
        v = silu(raw[slot, :, :, ch].astype(f32))
        act[slot, 1, :, :, ch] = v.astype(bf16)
        shifted[:, 8:40] = v
        act[slot, 0, :, :, ch] = shifted[:, 7:39].astype(bf16)
        act[slot, 2, :, :, ch] = shifted[:, 9:41].astype(bf16)

    def await_edges(slot, band):
        top, bottom = band % 32 != 0, band % 32 != 31
        for there, row, side in ((top, 0, 1), (bottom, 9, 0)):

            @pl.when(there)
            def _():
                pltpu.make_async_copy(late_raw.at[slot], raw.at[slot, row], recv_edge.at[slot, side]).wait()

            @pl.when(jnp.logical_not(there))
            def _():
                raw[slot, row] = late_raw_zero

    load_x.wait()
    for slot in (EVEN, ODD):
        await_edges(slot, h)
        for half in range(2):
            prepare(slot, half)

    load_clips.wait()
    one, two = clips[0], clips[0] + clips[1]
    three = two + clips[2]

    def age(frame):
        begin = jnp.where(three <= frame, three, jnp.where(two <= frame, two, jnp.where(one <= frame, one, 0)))
        return frame - begin

    ages = [age((2 * s + 1 + d) % 16) for d in range(4)]
    lags = [[jnp.minimum(k, a) for k in range(3)] for a in ages]
    source = [[ODD - lags[0][k] for k in range(3)], [NEXT - lags[1][k] for k in range(3)]]
    source[0][0], source[1][0] = ODD, NEXT

    acc[...] = jnp.zeros_like(acc)

    def add_taps(output, k, half):
        slot = source[output][k]
        ch = slice(half * 256, half * 256 + 256)
        lhs = jnp.concatenate(
            [act[slot, j, i : i + 8, :, ch].reshape(256, 256) for i in range(3) for j in range(3)], axis=1
        )
        rhs = wm[k, :, :, ch].reshape(9 * 256, 512)
        acc[output] += jnp.dot(lhs, rhs, preferred_element_type=f32)

    load_w[0].wait()
    add_taps(0, 0, 0)
    add_taps(0, 0, 1)
    load_w[1].wait()
    add_taps(0, 1, 0)
    pl.semaphore_wait(know_plane, 7)
    for d in (-4, -3, -2, -1, 1, 2, 3, 4):
        pl.semaphore_signal(know_four, inc=1, device_id=along_z(d), device_id_type=MESH)
    add_taps(0, 1, 1)
    load_w[2].wait()
    await_edges(NEXT, band_next)
    await_edges(PREV, band_prev)
    for half in range(2):
        main[2 * half].wait_recv()
        main[2 * half + 1].wait_recv()
        prepare(NEXT, half)
        prepare(PREV, half)
        add_taps(0, 2, half)
        add_taps(1, 0, half)
        if half == 1:
            pl.semaphore_wait(know_four, 8)
            for d in (-4, 4):
                pl.semaphore_signal(know_all, inc=1, device_id=along_z(d), device_id_type=MESH)
        add_taps(1, 1, half)
        add_taps(1, 2, half)
    pl.semaphore_wait(know_all, 2)

    @pl.when(h == 32)
    def _():
        for c in edge_copies(0, True):
            c.start()

    @pl.when(h == 31)
    def _():
        for c in edge_copies(1, True):
            c.start()

    def is_edge(band):
        return jnp.logical_or(band == 31, band == 32)

    late_slots = ((EVEN, is_edge(h)), (ODD, is_edge(h)), (NEXT, is_edge(band_next)), (PREV, is_edge(band_prev)))

    @pl.when(jnp.logical_or(is_edge(h), is_edge(other)))
    def _():
        at_bottom = h % 32 == 31
        for slot, is_late in late_slots:

            @pl.when(jnp.logical_and(is_late, at_bottom))
            def _():
                pltpu.make_async_copy(late_raw.at[slot], late_raw.at[slot], recv_edge.at[slot, 0]).wait()

            @pl.when(jnp.logical_and(is_late, jnp.logical_not(at_bottom)))
            def _():
                pltpu.make_async_copy(late_raw.at[slot], late_raw.at[slot], recv_edge.at[slot, 1]).wait()

            @pl.when(jnp.logical_not(is_late))
            def _():
                late_raw[slot] = late_raw_zero

        for half in range(2):
            ch = slice(half * 256, half * 256 + 256)
            v = silu(late_raw[:, :, ch].astype(f32))
            late[:, 1, :, ch] = v.astype(bf16)
            shifted[0:4, 8:40] = v
            late[:, 0, :, ch] = shifted[0:4, 7:39].astype(bf16)
            late[:, 2, :, ch] = shifted[0:4, 9:41].astype(bf16)
        row = jnp.where(at_bottom, 7, 0)
        tap = jnp.where(at_bottom, 2, 0)
        total = None
        for k in range(3):
            lhs = jnp.concatenate(
                [jnp.concatenate([late[source[o][k], j] for j in range(3)], axis=1) for o in range(2)], axis=0
            )
            part = jnp.dot(lhs, wm[k, tap].reshape(3 * 512, 512), preferred_element_type=f32)
            total = part if total is None else total + part
        acc[:, pl.ds(pl.multiple_of(row * 32, 32), 32)] += total.reshape(2, 32, 512)

    small[0].wait()
    for output, slot in ((0, ODD), (1, NEXT)):
        here = raw[slot, 1:9].reshape(256, 512).astype(f32)
        hidden = (here + acc[output] + bm[...]).astype(bf16).astype(f32)
        act2[output] = silu(hidden).astype(bf16)

    for c in tap_copies:
        c.wait()
    conv2[:, :, :, 0:8] = jnp.zeros((3, 3, 16, 8, 128), f32)
    conv2[:, :, :, 40:48] = jnp.zeros((3, 3, 16, 8, 128), f32)
    for j in range(3):
        product = lax.dot_general(
            act2[...].reshape(512, 512), wl[j], (((1,), (1,)), ((), ())), preferred_element_type=f32
        )
        for k in range(3):
            conv2[k, j, :, 8:40] = product[:, k * 128 : k * 128 + 128].reshape(16, 32, 128)
    lane = lax.broadcasted_iota(jnp.int32, (16, 128), 1)
    groups = [lane // 16 == n for n in range(8)]
    totals = [[[] for _ in range(3)] for _ in range(4)]
    for parity in range(2):
        for d in range(4):
            value = None
            for dest, output, lag, taps in ROUTES:
                if dest != d:
                    continue
                for k in taps:
                    keep = (lags[d][k] == lag).astype(f32)
                    summed = None
                    for j in range(3):
                        part = conv2[k, j, output * 8 : output * 8 + 8, pl.ds(7 + j + parity, 16, stride=2)]
                        summed = part if summed is None else summed + part
                    summed = summed * keep
                    value = summed if value is None else value + summed
            for r in range(8):
                for i in range(3):
                    place = r - i + 3
                    index, a = place // 2, place % 2
                    group = index // 3 * 4 + a * 2 + parity
                    turned = pltpu.roll(value[r], (group - i) * 16 % 128, 1)
                    totals[d][index % 3].append(jnp.where(groups[group], turned, 0.0))
    for d in range(4):
        for n in range(3):
            outgoing[d, n] = functools.reduce(lambda p, q: p + q, totals[d][n])

    small[2].wait()
    for d in range(4):
        frame = (2 * s + 1 + d) % 16
        band = h if d == 0 else band_next
        role = d // 2
        slot = band % 32
        side = band // 32

        def send(q, there_core, target, sems, mine):
            there = (frame // 2, (frame % 2) * 32 + 2 * q + there_core)
            src = outgoing.at[d, :, q]
            if not mine:
                pltpu.make_async_remote_copy(
                    src, target, sems[0], sems[1], device_id=there, device_id_type=MESH
                ).start()
                return
            is_self = jnp.logical_and(there[0] == s, there[1] == h)

            @pl.when(is_self)
            def _():
                pltpu.make_async_copy(src, target, sems[1]).start()

            @pl.when(jnp.logical_not(is_self))
            def _():
                pltpu.make_async_remote_copy(
                    src, target, sems[0], sems[1], device_id=there, device_id_type=MESH
                ).start()

        @pl.loop(0, 16)
        def _(q):
            send(q, side, incoming.at[role, :, slot], (send_patch.at[d], recv_patch.at[role]), d == 0)

        @pl.when(is_edge(band))
        def _():
            @pl.loop(0, 16)
            def _(q):
                send(q, 1 - side, incoming.at[role, :, 32], (send_extra.at[d], recv_extra.at[role]), d == 0)

    to = lax.broadcasted_iota(jnp.int32, (64, 64), 0)
    at = lax.broadcasted_iota(jnp.int32, (64, 64), 1)
    move = (at == (to % 16) * 4 + to // 16).astype(bf16)
    pwp[...] = jnp.dot(move, pw[...], preferred_element_type=f32).astype(bf16)
    small[1].wait()
    small[3].wait()

    for role in range(2):
        arrived = incoming.at[role, :, pl.ds(0, 32)]
        pltpu.make_async_copy(arrived, arrived, recv_patch.at[role]).wait()
        arrived = incoming.at[role, :, 32]
        pltpu.make_async_copy(arrived, arrived, recv_extra.at[role]).wait()
    total = incoming[0] + incoming[1]
    band_row = lax.broadcasted_iota(jnp.int32, (32, 64), 0)
    piece = [total[n % 3, 0:32, (n // 3) * 64 : (n // 3) * 64 + 64] for n in range(6)]
    extra = total[:, 32:33]
    before = jnp.where(core == 1, extra[2, :, 64:128], 0.0)
    after = jnp.where(core == 0, extra[0, :, 0:64], 0.0)
    piece[1] += jnp.where(band_row == 0, before, pltpu.roll(piece[5], 1, 0))
    piece[4] += jnp.where(band_row == 31, after, pltpu.roll(piece[0], 31, 0))
    for n in range(4):
        patches[pl.ds(n, 32, stride=4), 0:64] = piece[1 + n]
    bias = jnp.concatenate([bl[...]] * 4, axis=1)
    latent = ((patches[:, 0:64] + bias) * latent_scale).astype(bf16)
    out[...] = (jnp.dot(latent, pwp[...], preferred_element_type=f32) + pb[...]).astype(bf16)
    write = pltpu.make_async_copy(out, out_hbm, sem_out)
    write.start()

    for c in main:
        c.wait_send()
    for side, sends in ((0, h != 0), (1, h != 63)):

        @pl.when(sends)
        def _():
            for c in edge_copies(side, False):
                c.wait_send()

    for d in range(4):
        band = h if d == 0 else band_next
        if d == 0:
            own = jnp.logical_and(zh == 1, core == 1)
            own_extra = h == 32
        else:
            own = own_extra = None
        for sem, sent, one_less in ((send_patch.at[d], None, own), (send_extra.at[d], is_edge(band), own_extra)):
            whole, less = outgoing.at[d], outgoing.at[d, :, pl.ds(0, 15)]

            def finish(sem=sem, one_less=one_less, whole=whole, less=less):
                if one_less is None:
                    pltpu.make_async_copy(whole, whole, sem).wait()
                    return

                @pl.when(one_less)
                def _():
                    pltpu.make_async_copy(less, less, sem).wait()

                @pl.when(jnp.logical_not(one_less))
                def _():
                    pltpu.make_async_copy(whole, whole, sem).wait()

            if sent is None:
                finish()
            else:
                pl.when(sent)(finish)
    write.wait()


def per_device(features, clip_frames, conv_mid, bias_mid, conv_latent, bias_latent, patch_weight, patch_bias):
    dma, regular = pltpu.SemaphoreType.DMA, pltpu.SemaphoreType.REGULAR
    anywhere = pl.BlockSpec(memory_space=pl.ANY)
    return pl.pallas_call(
        kernel,
        out_shape=jax.ShapeDtypeStruct((128, 3072), bf16),
        in_specs=[anywhere] * 8,
        out_specs=anywhere,
        scratch_shapes=[
            pltpu.VMEM((4, 10, 32, 512), bf16),
            pltpu.VMEM((4, 3, 10, 32, 512), bf16),
            pltpu.VMEM((10, 48, 256), f32),
            pltpu.VMEM((3, 3, 3, 512, 512), bf16),
            pltpu.VMEM((2, 256, 512), f32),
            pltpu.VMEM((4, 32, 512), bf16),
            pltpu.VMEM((4, 3, 32, 512), bf16),
            pltpu.VMEM((2, 256, 512), bf16),
            pltpu.VMEM((3, 384, 512), bf16),
            pltpu.VMEM((3, 3, 16, 48, 128), f32),
            pltpu.VMEM((4, 3, 16, 128), f32),
            pltpu.VMEM((2, 3, 40, 128), f32),
            pltpu.VMEM((128, 128), f32),
            pltpu.VMEM((64, 3072), bf16),
            pltpu.VMEM((64, 3072), bf16),
            pltpu.VMEM((128, 3072), bf16),
            pltpu.VMEM((1, 512), f32),
            pltpu.VMEM((1, 16), f32),
            pltpu.VMEM((1, 3072), f32),
            pltpu.SMEM((4,), jnp.int32),
            dma, dma((3,)), dma((32,)), dma,
            dma((2, 2)), dma((2, 2)), dma((4, 2)), dma((4, 2)),
            dma((4,)), dma((2,)), dma((4,)), dma((2,)),
            regular, regular, regular,
        ],
        compiler_params=pltpu.CompilerParams(
            collective_id=0, has_side_effects=True, vmem_limit_bytes=58 * 2**20
        ),
    )(
        features, clip_frames, conv_mid, bias_mid.reshape(1, -1), jnp.swapaxes(conv_latent, 3, 4),
        bias_latent.reshape(1, -1), patch_weight, patch_bias.reshape(1, -1),
    )


def solution(mesh):
    return jax.shard_map(
        per_device,
        mesh=mesh,
        in_specs=(P("tm", "height", None, None), P(), P(), P(), P(), P(), P(), P()),
        out_specs=P(("tm", "height"), None),
        check_vma=False,
    )
```

time: 144 us -> 56.7 us (0.39); the launches traced: 142 us -> 56.6 us
  starting transfers between devices: 60.6 us -> 0 us
  Pallas kernels: 0 us -> 54.5 us
  waiting for transfers between devices: 35.5 us -> 0 us
  local copies, waits for them, and re-layouts: 22.3 us -> 2.06 us
  matrix products: 18.5 us -> 0 us
  other arithmetic: 4.01 us -> 0 us
    pallas_call x0 -> x1, Pallas kernels: none -> 54.5 us  [per_device(): pl.pallas_call(kernel, out_shape=jax.ShapeDtypeStruct((128, 3072), bf16),...]
    all_to_all x1 -> x0, starting transfers between devices: 41.2 us -> none  [per_device(): lax.all_to_all(outgoing, 'height', split_axis=0, concat_axis=0, tiled=True)]
    ppermute x6 -> x0, starting transfers between devices: 19.5 us -> none  [the longest x2 7.95 us: passed_along(): return lax.ppermute(x, axis, pairs)]
    ppermute x6 -> x0, waiting for transfers between devices: 19.1 us -> none  [the longest x2 13.3 us: passed_along(): return lax.ppermute(x, axis, pairs)]
    dot_general x7 -> x0, matrix products: 18.5 us -> none  [the longest x6 18.2 us: lagged_sum(): jnp.einsum('fhwk,ko->fhwo', picked, taps[back_step], preferred_element_ty...]
    all_to_all x1 -> x0, waiting for transfers between devices: 16.5 us -> none  [per_device(): lax.all_to_all(outgoing, 'height', split_axis=0, concat_axis=0, tiled=True)]
    slice x5 -> x0, local copies, waits for them, and re-layouts: 11.1 us -> none  [lagged_sum(): taps[back_step]]
    unnamed x42 -> x1, local copies, waits for them, and re-layouts: 5.95 us -> 2.06 us
  transfers between devices with their start and end apart: 7 -> 0, of which waited for: 4 -> 0; matrix products, arithmetic and copies ran while one was open for 10% -> 0% of each run, Pallas kernels for 0% -> 0%
where the time goes in v1:
time: 56.7 us; the launch traced here: 56.6 us
  Pallas kernels  54.5 us (96%)
  local copies, waits for them, and re-layouts  2.06 us (4%)
    pallas_call x1, Pallas kernels, per_device(): pl.pallas_call(kernel, out_shape=jax.ShapeDtypeStruct((128, 3072), bf16),...  54.5 us
    unnamed x1, local copies, waits for them, and re-layouts  2.06 us

profile of v1, /device:TPU:1, one launch (start us, length us, event | category | flops | bytes accessed | tf_op | source)
XLA Modules:
  0.0 56.6 jit_solution(5089488352639464799)
XLA Ops:
  0.0 54.5 %shard_map.82 = bf16[128,3072]{1,0:T(8,128)(2,1)} custom-call(bf16[2,8,32,512]{3,2,1,0:T(8,128)(2,1)} %x_hbm.1, s32[4]{0:T(128)} %clips_hbm.1, bf16[3,3,3,512,512]{4,3,2,1,0:T(8,128)(2,1)} %wm_hbm.1, f32[1,512]{1,0:T(1,128)} %bitcast.6, bf16[3,3,3,16,512]{4,3,2,1,0:T(8,128)(2,1)} %bitcast.4, f32[1,16]{1,0:T(1,128)} %bitcast.7, bf16[64,3072]{1,0:T(8,128)(2,1)} %pw_hbm.1, ...), custom_call_target="tpu_custom_call" | custom-call | tf_op jit(solution)/shard_map/pallas_call | solution.py:423
  54.5 2.1 %copy.10 = bf16[128,3072]{1,0:T(8,128)(2,1)} copy(bf16[128,3072]{1,0:T(8,128)(2,1)} %shard_map.82) | data formatting | bytes 1572864

commit v2 on v1

--- a/solution.py
+++ b/solution.py
@@ -27,10 +27,10 @@
 
 
 def kernel(
-    x_hbm, clips_hbm, wm_hbm, bm_hbm, wl_hbm, bl_hbm, pw_hbm, pb_hbm, out_hbm,
-    raw, act, shifted, wm, acc, late_raw, late, act2, wl, conv2, outgoing, incoming, patches, pw, pwp, out, bm, bl, pb, clips,
+    x_hbm, clips_hbm, wm_hbm, bm_hbm, wl_hbm, bl_hbm, out_hbm,
+    raw, act, shifted, wm, acc, late_raw, late, act2, taps, wl, conv2, outgoing, incoming, patches, out, bm, bl, clips,
     sem_x, sem_w, sem_small, sem_out, send_main, recv_main, send_edge, recv_edge, send_patch, recv_patch, send_extra, recv_extra,
-    know_plane, know_four, know_all,
+    know_plane, know_four, know_all, know_column, know_corners,
 ):
     s, h = lax.axis_index("tm"), lax.axis_index("height")
     zh, y, x, core = h // 32, (h // 8) % 4, (h // 2) % 4, h % 2
@@ -55,10 +55,11 @@
 
     load_x = pltpu.make_async_copy(x_hbm, raw.at[pl.ds(EVEN, 2), pl.ds(1, 8)], sem_x)
     load_x.start()
-    load_w = [pltpu.make_async_copy(wm_hbm.at[k], wm.at[k], sem_w.at[k]) for k in range(3)]
+    load_w = [pltpu.make_async_copy(wm_hbm.at[k, i], wm.at[k, i], sem_w.at[3 * k + i]) for k in range(3) for i in range(3)]
     load_clips = pltpu.make_async_copy(clips_hbm, clips, sem_small.at[0])
     load_clips.start()
-    load_w[0].start()
+    for c in load_w[:3]:
+        c.start()
 
     line = [device(s, zh, y, (x + d) % 4, c) for d in (1, 2, 3) for c in (0, 1)] + [device(s, zh, y, x, 1 - core)]
     column = [device(s, zh, (y + d) % 4, x, core) for d in (1, 2, 3)]
@@ -69,15 +70,23 @@
 
     @pl.when(has_top)
     def _():
-        for there in above(-1):
+        pl.semaphore_signal(barrier, inc=1, device_id=above(-1)[0], device_id_type=MESH)
+
+    @pl.when(has_bottom)
+    def _():
+        pl.semaphore_signal(barrier, inc=1, device_id=above(1)[0], device_id_type=MESH)
+
+    at_corner = jnp.logical_or(h % 32 == 0, h % 32 == 31)
+    opposite = (s, zh * 32 + 31 - h % 32)
+    corner_z = [along_z(d) for d in (-4, -3, 3, 4)]
+
+    @pl.when(at_corner)
+    def _():
+        for there in corner_z + [opposite]:
             pl.semaphore_signal(barrier, inc=1, device_id=there, device_id_type=MESH)
 
-    @pl.when(has_bottom)
-    def _():
-        for there in above(1):
-            pl.semaphore_signal(barrier, inc=1, device_id=there, device_id_type=MESH)
-
-    pl.semaphore_wait(barrier, 14 + 3 * has_top.astype(jnp.int32) + 3 * has_bottom.astype(jnp.int32))
+    neighbours = 14 + has_top.astype(jnp.int32) + has_bottom.astype(jnp.int32) + 5 * at_corner.astype(jnp.int32)
+    pl.semaphore_wait(barrier, neighbours)
 
     main = []
     for half in range(2):
@@ -94,7 +103,8 @@
         here, lower, upper = above(2 * side - 1)
         row, there_row = (0, 9) if side == 0 else (7, 0)
         copies = []
-        for slot, frame, there in ((EVEN, 0, here), (ODD, 1, here), (NEXT, 0, lower), (PREV, 1, upper)):
+        targets = ((EVEN, 0, here), (ODD, 1, here), (NEXT, 0, lower), (PREV, 1, upper))
+        for slot, frame, there in targets if to_late else targets[:2]:
             target = late_raw.at[slot] if to_late else raw.at[slot, there_row]
             copies.append(
                 pltpu.make_async_remote_copy(
@@ -104,6 +114,9 @@
             )
         return copies
 
+    for c in main[:2]:
+        c.start()
+
     @pl.when(has_top)
     def _():
         for c in edge_copies(0, False):
@@ -114,25 +127,22 @@
         for c in edge_copies(1, False):
             c.start()
 
-    for c in main:
-        c.start()
     for there in column + near_z:
         pl.semaphore_signal(know_plane, inc=1, device_id=there, device_id_type=MESH)
-    load_w[1].start()
-    load_w[2].start()
+
+    @pl.when(at_corner)
+    def _():
+        for there in near_z + corner_z + [opposite]:
+            pl.semaphore_signal(know_column, inc=1, device_id=there, device_id_type=MESH)
+
     small = [
         pltpu.make_async_copy(a, b, sem_small.at[1 + i])
-        for i, (a, b) in enumerate(((bm_hbm, bm), (bl_hbm, bl), (pw_hbm, pw), (pb_hbm, pb)))
+        for i, (a, b) in enumerate(((bm_hbm, bm), (bl_hbm, bl)))
     ]
     for c in small:
         c.start()
-    wl[...] = jnp.zeros_like(wl)
-    tap_copies = [
-        pltpu.make_async_copy(wl_hbm.at[k, i, j], wl.at[j, pl.ds(k * 128 + i * 16, 16)], sem_small.at[5 + k * 9 + i * 3 + j])
-        for k in range(3) for i in range(3) for j in range(3)
-    ]
-    for c in tap_copies:
-        c.start()
+    load_taps = pltpu.make_async_copy(wl_hbm, taps, sem_small.at[3])
+    load_taps.start()
 
     shifted[:, 0:8] = jnp.zeros((10, 8, 256), f32)
     shifted[:, 40:48] = jnp.zeros((10, 8, 256), f32)
@@ -149,6 +159,16 @@
         act[slot, 0, :, :, ch] = shifted[:, 7:39].astype(bf16)
         act[slot, 2, :, :, ch] = shifted[:, 9:41].astype(bf16)
 
+    def forwards(side):
+        row = 9 if side == 0 else 0
+        return [
+            pltpu.make_async_remote_copy(
+                raw.at[slot, row], raw.at[to, row], send_edge.at[to, side], recv_edge.at[to, side],
+                device_id=there, device_id_type=MESH,
+            )
+            for slot, to, there in ((EVEN, NEXT, down), (ODD, PREV, up))
+        ]
+
     def await_edges(slot, band):
         top, bottom = band % 32 != 0, band % 32 != 31
         for there, row, side in ((top, 0, 1), (bottom, 9, 0)):
@@ -161,11 +181,12 @@
             def _():
                 raw[slot, row] = late_raw_zero
 
-    load_x.wait()
-    for slot in (EVEN, ODD):
-        await_edges(slot, h)
-        for half in range(2):
-            prepare(slot, half)
+    wl[...] = jnp.zeros_like(wl)
+    load_taps.wait()
+    for k in range(3):
+        for i in range(3):
+            for j in range(3):
+                wl[j, k * 128 + i * 16 : k * 128 + i * 16 + 16] = taps[k, i, j]
 
     load_clips.wait()
     one, two = clips[0], clips[0] + clips[1]
@@ -180,7 +201,34 @@
     source = [[ODD - lags[0][k] for k in range(3)], [NEXT - lags[1][k] for k in range(3)]]
     source[0][0], source[1][0] = ODD, NEXT
 
+    for first, second in ((main[0], main[2]), (main[1], main[3])):
+        first.wait_send()
+        second.start()
+    pl.semaphore_wait(know_plane, 7)
+    for there in near_z + corner_z:
+        pl.semaphore_signal(know_four, inc=1, device_id=there, device_id_type=MESH)
+
+    load_x.wait()
+    await_edges(EVEN, h)
+    await_edges(ODD, h)
+    for side, there in ((0, has_bottom), (1, has_top)):
+
+        @pl.when(there)
+        def _():
+            for c in forwards(side):
+                c.start()
+
+    for slot in (ODD, EVEN):
+        for half in range(2):
+            prepare(slot, half)
+
     acc[...] = jnp.zeros_like(acc)
+
+    def await_weights(k):
+        for n in range(3 * k, 3 * k + 3):
+            load_w[n].wait()
+            if n + 3 < 9:
+                load_w[n + 3].start()
 
     def add_taps(output, k, half):
         slot = source[output][k]
@@ -191,16 +239,23 @@
         rhs = wm[k, :, :, ch].reshape(9 * 256, 512)
         acc[output] += jnp.dot(lhs, rhs, preferred_element_type=f32)
 
-    load_w[0].wait()
+    await_weights(0)
     add_taps(0, 0, 0)
     add_taps(0, 0, 1)
-    load_w[1].wait()
+    await_weights(1)
     add_taps(0, 1, 0)
-    pl.semaphore_wait(know_plane, 7)
-    for d in (-4, -3, -2, -1, 1, 2, 3, 4):
-        pl.semaphore_signal(know_four, inc=1, device_id=along_z(d), device_id_type=MESH)
     add_taps(0, 1, 1)
-    load_w[2].wait()
+    pl.semaphore_wait(know_four, 8)
+    for there in (corner_z[0], corner_z[3]):
+        pl.semaphore_signal(know_all, inc=1, device_id=there, device_id_type=MESH)
+
+    @pl.when(at_corner)
+    def _():
+        pl.semaphore_wait(know_column, 9)
+        for there in (corner_z[0], corner_z[3]):
+            pl.semaphore_signal(know_corners, inc=1, device_id=there, device_id_type=MESH)
+
+    await_weights(2)
     await_edges(NEXT, band_next)
     await_edges(PREV, band_prev)
     for half in range(2):
@@ -210,23 +265,23 @@
         prepare(PREV, half)
         add_taps(0, 2, half)
         add_taps(1, 0, half)
-        if half == 1:
-            pl.semaphore_wait(know_four, 8)
-            for d in (-4, 4):
-                pl.semaphore_signal(know_all, inc=1, device_id=along_z(d), device_id_type=MESH)
         add_taps(1, 1, half)
         add_taps(1, 2, half)
+        if half == 1:
+            continue
+
+        @pl.when(at_corner)
+        def _():
+            pl.semaphore_wait(know_corners, 2)
+
+        for side, far in ((0, 32), (1, 31)):
+
+            @pl.when(h == far)
+            def _():
+                for c in edge_copies(side, True):
+                    c.start()
+
     pl.semaphore_wait(know_all, 2)
-
-    @pl.when(h == 32)
-    def _():
-        for c in edge_copies(0, True):
-            c.start()
-
-    @pl.when(h == 31)
-    def _():
-        for c in edge_copies(1, True):
-            c.start()
 
     def is_edge(band):
         return jnp.logical_or(band == 31, band == 32)
@@ -274,8 +329,6 @@
         hidden = (here + acc[output] + bm[...]).astype(bf16).astype(f32)
         act2[output] = silu(hidden).astype(bf16)
 
-    for c in tap_copies:
-        c.wait()
     conv2[:, :, :, 0:8] = jnp.zeros((3, 3, 16, 8, 128), f32)
     conv2[:, :, :, 40:48] = jnp.zeros((3, 3, 16, 8, 128), f32)
     for j in range(3):
@@ -312,7 +365,6 @@
         for n in range(3):
             outgoing[d, n] = functools.reduce(lambda p, q: p + q, totals[d][n])
 
-    small[2].wait()
     for d in range(4):
         frame = (2 * s + 1 + d) % 16
         band = h if d == 0 else band_next
@@ -350,12 +402,7 @@
             def _(q):
                 send(q, 1 - side, incoming.at[role, :, 32], (send_extra.at[d], recv_extra.at[role]), d == 0)
 
-    to = lax.broadcasted_iota(jnp.int32, (64, 64), 0)
-    at = lax.broadcasted_iota(jnp.int32, (64, 64), 1)
-    move = (at == (to % 16) * 4 + to // 16).astype(bf16)
-    pwp[...] = jnp.dot(move, pw[...], preferred_element_type=f32).astype(bf16)
     small[1].wait()
-    small[3].wait()
 
     for role in range(2):
         arrived = incoming.at[role, :, pl.ds(0, 32)]
@@ -374,17 +421,34 @@
         patches[pl.ds(n, 32, stride=4), 0:64] = piece[1 + n]
     bias = jnp.concatenate([bl[...]] * 4, axis=1)
     latent = ((patches[:, 0:64] + bias) * latent_scale).astype(bf16)
-    out[...] = (jnp.dot(latent, pwp[...], preferred_element_type=f32) + pb[...]).astype(bf16)
+    at = lax.broadcasted_iota(jnp.int32, (64, 64), 0)
+    to = lax.broadcasted_iota(jnp.int32, (64, 64), 1)
+    move = (to == (at % 16) * 4 + at // 16).astype(bf16)
+    out[...] = jnp.dot(latent, move, preferred_element_type=f32).astype(bf16)
     write = pltpu.make_async_copy(out, out_hbm, sem_out)
     write.start()
 
-    for c in main:
+    for c in main[2:]:
         c.wait_send()
+    for side, there in ((0, has_bottom), (1, has_top)):
+
+        @pl.when(there)
+        def _():
+            for c in forwards(side):
+                c.wait_send()
+
     for side, sends in ((0, h != 0), (1, h != 63)):
 
         @pl.when(sends)
         def _():
             for c in edge_copies(side, False):
+                c.wait_send()
+
+    for side, far in ((0, 32), (1, 31)):
+
+        @pl.when(h == far)
+        def _():
+            for c in edge_copies(side, True)[2:]:
                 c.wait_send()
 
     for d in range(4):
@@ -420,10 +484,10 @@
 def per_device(features, clip_frames, conv_mid, bias_mid, conv_latent, bias_latent, patch_weight, patch_bias):
     dma, regular = pltpu.SemaphoreType.DMA, pltpu.SemaphoreType.REGULAR
     anywhere = pl.BlockSpec(memory_space=pl.ANY)
-    return pl.pallas_call(
+    latent_patches = pl.pallas_call(
         kernel,
-        out_shape=jax.ShapeDtypeStruct((128, 3072), bf16),
-        in_specs=[anywhere] * 8,
+        out_shape=jax.ShapeDtypeStruct((128, 64), bf16),
+        in_specs=[anywhere] * 6,
         out_specs=anywhere,
         scratch_shapes=[
             pltpu.VMEM((4, 10, 32, 512), bf16),
@@ -434,30 +498,30 @@
             pltpu.VMEM((4, 32, 512), bf16),
             pltpu.VMEM((4, 3, 32, 512), bf16),
             pltpu.VMEM((2, 256, 512), bf16),
+            pltpu.VMEM((3, 3, 3, 16, 512), bf16),
             pltpu.VMEM((3, 384, 512), bf16),
             pltpu.VMEM((3, 3, 16, 48, 128), f32),
             pltpu.VMEM((4, 3, 16, 128), f32),
             pltpu.VMEM((2, 3, 40, 128), f32),
             pltpu.VMEM((128, 128), f32),
-            pltpu.VMEM((64, 3072), bf16),
-            pltpu.VMEM((64, 3072), bf16),
-            pltpu.VMEM((128, 3072), bf16),
+            pltpu.VMEM((128, 64), bf16),
             pltpu.VMEM((1, 512), f32),
             pltpu.VMEM((1, 16), f32),
-            pltpu.VMEM((1, 3072), f32),
             pltpu.SMEM((4,), jnp.int32),
-            dma, dma((3,)), dma((32,)), dma,
+            dma, dma((9,)), dma((4,)), dma,
             dma((2, 2)), dma((2, 2)), dma((4, 2)), dma((4, 2)),
             dma((4,)), dma((2,)), dma((4,)), dma((2,)),
-            regular, regular, regular,
+            regular, regular, regular, regular, regular,
         ],
         compiler_params=pltpu.CompilerParams(
             collective_id=0, has_side_effects=True, vmem_limit_bytes=58 * 2**20
         ),
     )(
         features, clip_frames, conv_mid, bias_mid.reshape(1, -1), jnp.swapaxes(conv_latent, 3, 4),
-        bias_latent.reshape(1, -1), patch_weight, patch_bias.reshape(1, -1),
+        bias_latent.reshape(1, -1),
     )
+    product = jnp.dot(latent_patches, patch_weight, preferred_element_type=f32)
+    return (product + patch_bias).astype(bf16)
 
 
 def solution(mesh):

time: 56.7 us -> 55.8 us (0.984)
  local copies, waits for them, and re-layouts: 2.06 us -> 0.01 us
  matrix products: 0 us -> 1.99 us
  Pallas kernels: 54.5 us -> 53.6 us
    unnamed x1 -> x4, local copies, waits for them, and re-layouts: 2.06 us -> 0.01 us
    dot_general x0 -> x1, matrix products: none -> 1.99 us  [per_device(): product = jnp.dot(latent_patches, patch_weight, preferred_element_type=f32)]
    pallas_call x1, Pallas kernels: 54.5 us -> 53.6 us  [per_device(): pl.pallas_call(kernel, out_shape=jax.ShapeDtypeStruct((128, 64), bf16), i...]
where the time goes in v2:
time: 55.8 us; the launch traced here: 55.6 us
  Pallas kernels  53.6 us (96%)
  matrix products  1.99 us (4%)
    pallas_call x1, Pallas kernels, per_device(): pl.pallas_call(kernel, out_shape=jax.ShapeDtypeStruct((128, 64), bf16), i...  53.6 us
    dot_general x1, matrix products, per_device(): product = jnp.dot(latent_patches, patch_weight, preferred_element_type=f32)  1.99 us

profile of v2, /device:TPU:1, one launch (start us, length us, event | category | flops | bytes accessed | tf_op | source)
XLA Modules:
  0.0 55.6 jit_solution(990044336928347946)
XLA Ops:
  0.0 0.0 copy-start
  0.0 0.0 copy-start.1
  0.0 53.6 %shard_map.82 = bf16[128,64]{1,0:T(8,128)(2,1)} custom-call(bf16[2,8,32,512]{3,2,1,0:T(8,128)(2,1)} %x_hbm.1, s32[4]{0:T(128)} %clips_hbm.1, bf16[3,3,3,512,512]{4,3,2,1,0:T(8,128)(2,1)} %wm_hbm.1, f32[1,512]{1,0:T(1,128)} %bitcast.6, bf16[3,3,3,16,512]{4,3,2,1,0:T(8,128)(2,1)} %bitcast.5, f32[1,16]{1,0:T(1,128)} %bitcast.7), custom_call_target="tpu_custom_call" | custom-call | tf_op jit(solution)/shard_map/pallas_call | solution.py:487
  53.6 0.0 copy-done
  53.6 0.0 copy-done.1
  53.7 2.0 %fusion = bf16[128,3072]{1,0:T(8,128)(2,1)} fusion(bf16[128,64]{1,0:T(8,128)(2,1)} %shard_map.82, bf16[64,3072]{1,0:T(8,128)(2,1)S(1)} %copy-done, f32[3072]{0:T(1024)S(1)} %copy-done.1), kind=kOutput, calls=%fused_computation.1 | convolution fusion | flops 51118080 | bytes 1208320 | tf_op jit(solution)/shard_map/dot_general | solution.py:523
Async XLA Ops:
  0.0 53.6 %copy-start = (bf16[64,3072]{1,0:T(8,128)(2,1)S(1)}, bf16[64,3072]{1,0:T(8,128)(2,1)}, u32[]{:S(2)}) copy-start(bf16[64,3072]{1,0:T(8,128)(2,1)} %param.14) | copy-start | bytes 1179652
  0.0 53.6 %copy-start.1 = (f32[3072]{0:T(1024)S(1)}, f32[3072]{0:T(1024)}, u32[]{:S(2)}) copy-start(f32[3072]{0:T(1024)} %param.15) | copy-start | bytes 36868

commit v3 on v2

--- a/solution.py
+++ b/solution.py
@@ -151,13 +151,14 @@
     def silu(v):
         return v / (1.0 + jnp.exp(-v))
 
-    def prepare(slot, half):
+    def prepare(slot, half, first, last):
         ch = slice(half * 256, half * 256 + 256)
-        v = silu(raw[slot, :, :, ch].astype(f32))
-        act[slot, 1, :, :, ch] = v.astype(bf16)
-        shifted[:, 8:40] = v
-        act[slot, 0, :, :, ch] = shifted[:, 7:39].astype(bf16)
-        act[slot, 2, :, :, ch] = shifted[:, 9:41].astype(bf16)
+        rows = slice(first, last)
+        v = silu(raw[slot, rows, :, ch].astype(f32))
+        act[slot, 1, rows, :, ch] = v.astype(bf16)
+        shifted[rows, 8:40] = v
+        act[slot, 0, rows, :, ch] = shifted[rows, 7:39].astype(bf16)
+        act[slot, 2, rows, :, ch] = shifted[rows, 9:41].astype(bf16)
 
     def forwards(side):
         row = 9 if side == 0 else 0
@@ -201,27 +202,6 @@
     source = [[ODD - lags[0][k] for k in range(3)], [NEXT - lags[1][k] for k in range(3)]]
     source[0][0], source[1][0] = ODD, NEXT
 
-    for first, second in ((main[0], main[2]), (main[1], main[3])):
-        first.wait_send()
-        second.start()
-    pl.semaphore_wait(know_plane, 7)
-    for there in near_z + corner_z:
-        pl.semaphore_signal(know_four, inc=1, device_id=there, device_id_type=MESH)
-
-    load_x.wait()
-    await_edges(EVEN, h)
-    await_edges(ODD, h)
-    for side, there in ((0, has_bottom), (1, has_top)):
-
-        @pl.when(there)
-        def _():
-            for c in forwards(side):
-                c.start()
-
-    for slot in (ODD, EVEN):
-        for half in range(2):
-            prepare(slot, half)
-
     acc[...] = jnp.zeros_like(acc)
 
     def await_weights(k):
@@ -229,6 +209,12 @@
             load_w[n].wait()
             if n + 3 < 9:
                 load_w[n + 3].start()
+
+    def add_rows(output, k, rows):
+        slot = source[output][k]
+        lhs = jnp.concatenate([act[slot, j, i : i + 8].reshape(256, 512) for i in rows for j in range(3)], axis=1)
+        rhs = jnp.concatenate([wm[k, i].reshape(3 * 512, 512) for i in rows], axis=0)
+        acc[output] += jnp.dot(lhs, rhs, preferred_element_type=f32)
 
     def add_taps(output, k, half):
         slot = source[output][k]
@@ -239,21 +225,56 @@
         rhs = wm[k, :, :, ch].reshape(9 * 256, 512)
         acc[output] += jnp.dot(lhs, rhs, preferred_element_type=f32)
 
+    load_x.wait()
+    for slot in (ODD, EVEN):
+        for half in range(2):
+            prepare(slot, half, 1, 9)
     await_weights(0)
-    add_taps(0, 0, 0)
-    add_taps(0, 0, 1)
+    add_rows(0, 0, (1,))
+    for c in main[2:]:
+        c.start()
     await_weights(1)
-    add_taps(0, 1, 0)
-    add_taps(0, 1, 1)
+    add_rows(0, 1, (1,))
+    pl.semaphore_wait(know_plane, 7)
+    for there in near_z + corner_z:
+        pl.semaphore_signal(know_four, inc=1, device_id=there, device_id_type=MESH)
+
+    @pl.when(at_corner)
+    def _():
+        pl.semaphore_wait(know_column, 9)
+        for there in (corner_z[0], corner_z[3]):
+            pl.semaphore_signal(know_corners, inc=1, device_id=there, device_id_type=MESH)
+
+    await_edges(EVEN, h)
+    await_edges(ODD, h)
+    for side, there in ((0, has_bottom), (1, has_top)):
+
+        @pl.when(there)
+        def _():
+            for c in forwards(side):
+                c.start()
+
+    for slot in (ODD, EVEN):
+        for half in range(2):
+            prepare(slot, half, 0, 1)
+            prepare(slot, half, 9, 10)
+    add_rows(0, 0, (0, 2))
+
+    @pl.when(at_corner)
+    def _():
+        pl.semaphore_wait(know_corners, 2)
+
+    for side, far in ((0, 32), (1, 31)):
+
+        @pl.when(h == far)
+        def _():
+            for c in edge_copies(side, True):
+                c.start()
+
+    add_rows(0, 1, (0, 2))
     pl.semaphore_wait(know_four, 8)
     for there in (corner_z[0], corner_z[3]):
         pl.semaphore_signal(know_all, inc=1, device_id=there, device_id_type=MESH)
-
-    @pl.when(at_corner)
-    def _():
-        pl.semaphore_wait(know_column, 9)
-        for there in (corner_z[0], corner_z[3]):
-            pl.semaphore_signal(know_corners, inc=1, device_id=there, device_id_type=MESH)
 
     await_weights(2)
     await_edges(NEXT, band_next)
@@ -261,26 +282,12 @@
     for half in range(2):
         main[2 * half].wait_recv()
         main[2 * half + 1].wait_recv()
-        prepare(NEXT, half)
-        prepare(PREV, half)
+        prepare(NEXT, half, 0, 10)
+        prepare(PREV, half, 0, 10)
         add_taps(0, 2, half)
         add_taps(1, 0, half)
         add_taps(1, 1, half)
         add_taps(1, 2, half)
-        if half == 1:
-            continue
-
-        @pl.when(at_corner)
-        def _():
-            pl.semaphore_wait(know_corners, 2)
-
-        for side, far in ((0, 32), (1, 31)):
-
-            @pl.when(h == far)
-            def _():
-                for c in edge_copies(side, True):
-                    c.start()
-
     pl.semaphore_wait(know_all, 2)
 
     def is_edge(band):
@@ -428,7 +435,7 @@
     write = pltpu.make_async_copy(out, out_hbm, sem_out)
     write.start()
 
-    for c in main[2:]:
+    for c in main:
         c.wait_send()
     for side, there in ((0, has_bottom), (1, has_top)):
 

time: 55.8 us -> 52.3 us (0.937)
  Pallas kernels: 53.6 us -> 50.1 us
    pallas_call x1, Pallas kernels: 53.6 us -> 50.1 us  [per_device(): pl.pallas_call(kernel, out_shape=jax.ShapeDtypeStruct((128, 64), bf16), i...]
where the time goes in v3:
time: 52.3 us; the launch traced here: 52.1 us
  Pallas kernels  50.1 us (96%)
  matrix products  1.99 us (4%)
    pallas_call x1, Pallas kernels, per_device(): pl.pallas_call(kernel, out_shape=jax.ShapeDtypeStruct((128, 64), bf16), i...  50.1 us
    dot_general x1, matrix products, per_device(): product = jnp.dot(latent_patches, patch_weight, preferred_element_type=f32)  1.99 us

profile of v3, /device:TPU:1, one launch (start us, length us, event | category | flops | bytes accessed | tf_op | source)
XLA Modules:
  0.0 52.1 jit_solution(15294786726040428339)
XLA Ops:
  0.0 0.0 copy-start
  0.0 0.0 copy-start.1
  0.0 50.1 %shard_map.82 = bf16[128,64]{1,0:T(8,128)(2,1)} custom-call(bf16[2,8,32,512]{3,2,1,0:T(8,128)(2,1)} %x_hbm.1, s32[4]{0:T(128)} %clips_hbm.1, bf16[3,3,3,512,512]{4,3,2,1,0:T(8,128)(2,1)} %wm_hbm.1, f32[1,512]{1,0:T(1,128)} %bitcast.6, bf16[3,3,3,16,512]{4,3,2,1,0:T(8,128)(2,1)} %bitcast.5, f32[1,16]{1,0:T(1,128)} %bitcast.7), custom_call_target="tpu_custom_call" | custom-call | tf_op jit(solution)/shard_map/pallas_call | solution.py:494
  50.1 0.0 copy-done
  50.1 0.0 copy-done.1
  50.1 2.0 %fusion = bf16[128,3072]{1,0:T(8,128)(2,1)} fusion(bf16[128,64]{1,0:T(8,128)(2,1)} %shard_map.82, bf16[64,3072]{1,0:T(8,128)(2,1)S(1)} %copy-done, f32[3072]{0:T(1024)S(1)} %copy-done.1), kind=kOutput, calls=%fused_computation.1 | convolution fusion | flops 51118080 | bytes 1208320 | tf_op jit(solution)/shard_map/dot_general | solution.py:530
Async XLA Ops:
  0.0 50.1 %copy-start = (bf16[64,3072]{1,0:T(8,128)(2,1)S(1)}, bf16[64,3072]{1,0:T(8,128)(2,1)}, u32[]{:S(2)}) copy-start(bf16[64,3072]{1,0:T(8,128)(2,1)} %param.14) | copy-start | bytes 1179652
  0.0 50.1 %copy-start.1 = (f32[3072]{0:T(1024)S(1)}, f32[3072]{0:T(1024)}, u32[]{:S(2)}) copy-start(f32[3072]{0:T(1024)} %param.15) | copy-start | bytes 36868

commit v4 on v3

--- a/solution.py
+++ b/solution.py
@@ -58,7 +58,7 @@
     load_w = [pltpu.make_async_copy(wm_hbm.at[k, i], wm.at[k, i], sem_w.at[3 * k + i]) for k in range(3) for i in range(3)]
     load_clips = pltpu.make_async_copy(clips_hbm, clips, sem_small.at[0])
     load_clips.start()
-    for c in load_w[:3]:
+    for c in load_w[:5]:
         c.start()
 
     line = [device(s, zh, y, (x + d) % 4, c) for d in (1, 2, 3) for c in (0, 1)] + [device(s, zh, y, x, 1 - core)]
@@ -207,8 +207,8 @@
     def await_weights(k):
         for n in range(3 * k, 3 * k + 3):
             load_w[n].wait()
-            if n + 3 < 9:
-                load_w[n + 3].start()
+            if n + 5 < 9:
+                load_w[n + 5].start()
 
     def add_rows(output, k, rows):
         slot = source[output][k]

time: 52.3 us -> 52.6 us (level)
  no operation moved by 1% of the time
where the time goes in v4:
time: 52.6 us; the launch traced here: 52.5 us
  Pallas kernels  50.4 us (96%)
  matrix products  1.99 us (4%)
    pallas_call x1, Pallas kernels, per_device(): pl.pallas_call(kernel, out_shape=jax.ShapeDtypeStruct((128, 64), bf16), i...  50.4 us
    dot_general x1, matrix products, per_device(): product = jnp.dot(latent_patches, patch_weight, preferred_element_type=f32)  1.99 us

profile of v4, /device:TPU:1, one launch (start us, length us, event | category | flops | bytes accessed | tf_op | source)
XLA Modules:
  0.0 52.5 jit_solution(5715663831040241724)
XLA Ops:
  0.0 0.0 copy-start
  0.0 0.0 copy-start.1
  0.0 50.4 %shard_map.82 = bf16[128,64]{1,0:T(8,128)(2,1)} custom-call(bf16[2,8,32,512]{3,2,1,0:T(8,128)(2,1)} %x_hbm.1, s32[4]{0:T(128)} %clips_hbm.1, bf16[3,3,3,512,512]{4,3,2,1,0:T(8,128)(2,1)} %wm_hbm.1, f32[1,512]{1,0:T(1,128)} %bitcast.6, bf16[3,3,3,16,512]{4,3,2,1,0:T(8,128)(2,1)} %bitcast.5, f32[1,16]{1,0:T(1,128)} %bitcast.7), custom_call_target="tpu_custom_call" | custom-call | tf_op jit(solution)/shard_map/pallas_call | solution.py:494
  50.4 0.0 copy-done
  50.5 0.0 copy-done.1
  50.5 2.0 %fusion = bf16[128,3072]{1,0:T(8,128)(2,1)} fusion(bf16[128,64]{1,0:T(8,128)(2,1)} %shard_map.82, bf16[64,3072]{1,0:T(8,128)(2,1)S(1)} %copy-done, f32[3072]{0:T(1024)S(1)} %copy-done.1), kind=kOutput, calls=%fused_computation.1 | convolution fusion | flops 51118080 | bytes 1208320 | tf_op jit(solution)/shard_map/dot_general | solution.py:530
Async XLA Ops:
  0.0 50.4 %copy-start = (bf16[64,3072]{1,0:T(8,128)(2,1)S(1)}, bf16[64,3072]{1,0:T(8,128)(2,1)}, u32[]{:S(2)}) copy-start(bf16[64,3072]{1,0:T(8,128)(2,1)} %param.14) | copy-start | bytes 1179652
  0.0 50.5 %copy-start.1 = (f32[3072]{0:T(1024)S(1)}, f32[3072]{0:T(1024)}, u32[]{:S(2)}) copy-start(f32[3072]{0:T(1024)} %param.15) | copy-start | bytes 36868
